TPU v7x, 32 devices: a whole 2x2x4 slice. The times are simulated.
32 devices in a mesh: dp: 4 (over z), expert: 8 (over y, x, core).
Axes of the slice: x: 2, y: 2, z: 4, core: 2. Of those that a mesh axis runs over, the one named last changes fastest.
Arguments:
- first_out: bfloat16 [4096, 1024], P(('dp', 'expert')), may hold values from -6 to 6
- second_out: bfloat16 [4096, 1024], P(('dp', 'expert')), may hold values from -6 to 6
- first_grad: bfloat16 [4096, 1024], P(('dp', 'expert')), may hold values from -6 to 6
- second_grad: bfloat16 [4096, 1024], P(('dp', 'expert')), may hold values from -6 to 6
- routes: int32 [4096, 2], P(('dp', 'expert')), may hold values from 0 to 7, all different within a row; in each aligned block of 128 rows (0 to 127, 128 to 255, ...) at most 64 rows name the same one
- gate_values: float32 [4096, 2], P(('dp', 'expert')), may hold values from 0.1 to 1
- w_gate: bfloat16 [8, 1024, 768], P('expert', 'dp'), may hold values from -0.1875 to 0.1875
- w_up: bfloat16 [8, 1024, 768], P('expert', 'dp'), may hold values from -0.1875 to 0.1875
- w_down: bfloat16 [8, 1024, 768], P('expert', 'dp'), may hold values from -0.21875 to 0.21875
Outputs:
- second_in: bfloat16 [4096, 1024], P(('dp', 'expert'))
- first_total: bfloat16 [4096, 1024], P(('dp', 'expert'))
- gate_grad: float32 [4096, 2], P(('dp', 'expert'))
- w_down_grad: float32 [8, 1024, 768], P('expert', 'dp')
Inputs may be any that keep to these rules, and one draw needn't show every extreme that they name: `routes`: each row names 2 different experts. Among the 128 rows of one device no expert is named more than 64 times, and in every draw some device names some expert exactly 64 times.
All inputs are finite; a program needn't handle non-finite values.
Results may differ from a plain program's by a relative error of at most 0.0051.
Values may be sent and summed in bfloat16 or wider, within the bound.
A program may use at most 64 MiB of HBM per device.

v0:
```python
import math

import jax
import jax.numpy as jnp
from jax import lax
from jax.sharding import PartitionSpec as P


def expert_rows(rows_in, rows_cot, gate_mat, up_mat, down_mat):
    pre_gate = jnp.dot(rows_in, gate_mat, preferred_element_type=jnp.float32)
    pre_up = jnp.dot(rows_in, up_mat, preferred_element_type=jnp.float32)
    squashed = jax.nn.sigmoid(pre_gate)
    activated = pre_gate * squashed
    hidden = (activated * pre_up).astype(jnp.bfloat16)
    out_rows = lax.dot_general(
        hidden, down_mat, (((1,), (1,)), ((), ())), preferred_element_type=jnp.float32
    ).astype(jnp.bfloat16)
    hidden_cot = jnp.dot(rows_cot, down_mat, preferred_element_type=jnp.float32)
    gate_cot = (hidden_cot * pre_up * squashed * (1.0 + pre_gate * (1.0 - squashed))).astype(
        jnp.bfloat16
    )
    up_cot = (hidden_cot * activated).astype(jnp.bfloat16)
    input_cot = lax.dot_general(
        gate_cot, gate_mat, (((1,), (1,)), ((), ())), preferred_element_type=jnp.float32
    )
    input_cot = input_cot + lax.dot_general(
        up_cot, up_mat, (((1,), (1,)), ((), ())), preferred_element_type=jnp.float32
    )
    return (out_rows, input_cot.astype(jnp.bfloat16), hidden)


def to_slots(placing, assigned_rows):
    return lax.dot_general(
        placing, assigned_rows, (((0,), (0,)), ((), ())), preferred_element_type=jnp.float32
    ).astype(jnp.bfloat16)


def per_device(
    first_out, second_out, first_grad, second_grad, routes, gate_values, w_gate, w_up, w_down
):
    count_here = first_out.shape[0]
    feature_count = first_out.shape[1]
    top_count = routes.shape[1]
    owners = lax.axis_size("expert")
    groups = lax.axis_size("dp")
    capacity = min(count_here, 2 * count_here * top_count // owners)
    assigned = count_here * top_count
    slots_all = owners * capacity
    expert_ids = routes.reshape(assigned)
    onehot = (expert_ids[:, None] == jnp.arange(owners, dtype=jnp.int32)[None, :]).astype(jnp.int32)
    before = jnp.cumsum(onehot, axis=0) - onehot
    rank_in = jnp.sum(before * onehot, axis=1)
    slot_index = expert_ids * capacity + rank_in
    placing = (slot_index[:, None] == jnp.arange(slots_all, dtype=jnp.int32)[None, :]).astype(
        jnp.bfloat16
    )
    repeated = jnp.broadcast_to(
        first_out[:, None, :], (count_here, top_count, feature_count)
    ).reshape(assigned, feature_count)
    grad_repeated = jnp.broadcast_to(
        second_grad[:, None, :], (count_here, top_count, feature_count)
    ).reshape(assigned, feature_count)
    cot_rows = (gate_values.reshape(assigned)[:, None] * grad_repeated.astype(jnp.float32)).astype(
        jnp.bfloat16
    )
    send_input = to_slots(placing, repeated).reshape(owners, capacity, feature_count)
    send_cot = to_slots(placing, cot_rows).reshape(owners, capacity, feature_count)
    arrived_input, arrived_cot = (
        lax.all_to_all(send_input, "expert", split_axis=0, concat_axis=0, tiled=True),
        lax.all_to_all(send_cot, "expert", split_axis=0, concat_axis=0, tiled=True),
    )
    rows_in = arrived_input.reshape(slots_all, feature_count)
    rows_cot = arrived_cot.reshape(slots_all, feature_count)
    gate_full, up_full, down_full = (
        lax.all_gather(w_gate, "dp", axis=1, tiled=True),
        lax.all_gather(w_up, "dp", axis=1, tiled=True),
        lax.all_gather(w_down, "dp", axis=1, tiled=True),
    )
    down_mat = down_full[0]
    out_rows, input_cot, hidden = expert_rows(rows_in, rows_cot, gate_full[0], up_full[0], down_mat)
    grad_scale = 1.0 / math.sqrt(count_here * groups)
    partial_grad = lax.dot_general(
        rows_cot, hidden, (((0,), (0,)), ((), ())), preferred_element_type=jnp.float32
    )
    reduced = lax.psum_scatter(partial_grad, "dp", scatter_dimension=0, tiled=True)
    w_down_grad = (reduced * grad_scale)[None]
    back_out, back_cot = (
        lax.all_to_all(
            out_rows.reshape(owners, capacity, feature_count),
            "expert",
            split_axis=0,
            concat_axis=0,
            tiled=True,
        ),
        lax.all_to_all(
            input_cot.reshape(owners, capacity, feature_count),
            "expert",
            split_axis=0,
            concat_axis=0,
            tiled=True,
        ),
    )
    out_assigned = jnp.dot(
        placing, back_out.reshape(slots_all, feature_count), preferred_element_type=jnp.float32
    )
    cot_assigned = jnp.dot(
        placing, back_cot.reshape(slots_all, feature_count), preferred_element_type=jnp.float32
    )
    expert_out = out_assigned.reshape(count_here, top_count, feature_count)
    combined = jnp.sum(gate_values[:, :, None] * expert_out, axis=1)
    second_in = (second_out.astype(jnp.float32) - combined).astype(jnp.bfloat16)
    gate_grad = jnp.sum(second_grad.astype(jnp.float32)[:, None, :] * expert_out, axis=2)
    first_total = (
        first_grad.astype(jnp.float32)
        + jnp.sum(cot_assigned.reshape(count_here, top_count, feature_count), axis=1)
    ).astype(jnp.bfloat16)
    return (second_in, first_total, gate_grad, w_down_grad)


def solution(mesh):
    placed = (
        P(("dp", "expert"), None),
        P(("dp", "expert"), None),
        P(("dp", "expert"), None),
        P(("dp", "expert"), None),
        P(("dp", "expert"), None),
        P(("dp", "expert"), None),
        P("expert", "dp", None),
        P("expert", "dp", None),
        P("expert", "dp", None),
    )
    return jax.shard_map(
        per_device,
        mesh=mesh,
        in_specs=placed,
        out_specs=(
            P(("dp", "expert"), None),
            P(("dp", "expert"), None),
            P(("dp", "expert"), None),
            P("expert", "dp", None),
        ),
        check_vma=False,
    )
```

profile of v0, /device:TPU:0, one launch (start us, length us, event | category | flops | bytes accessed | tf_op | source)
XLA Modules:
  0.0 194.5 jit_solution(1298778992399914303)
XLA Ops:
  7.2 0.7 all-gather.4.cloned.1.call-update
  7.9 0.7 all-gather.6.cloned.1.call-update
  8.7 0.7 all-gather.8.cloned.1.call-update
  9.4 0.8 copy.20
  10.5 1.2 broadcast_in_dim.6
  11.9 0.6 reduce-window.6
  12.9 1.6 convolution_convert_fusion.1
  14.5 5.2 %all-to-all-start = ((bf16[8,64,1024]{2,1,0:T(8,128)(2,1)}), bf16[8,64,1024]{2,1,0:T(8,128)(2,1)S(1)}, u32[]{:S(2)}, u32[]{:S(2)}) async-start(bf16[8,64,1024]{2,1,0:T(8,128)(2,1)} %bitcast.3), calls=%async_computation | async-start | bytes 2097152 | tf_op jit(solution)/shard_map/all_to_all | solution.py:69
  19.9 0.7 convert_element_type.61
  20.9 1.5 convolution_convert_fusion
  22.4 12.6 %all-to-all-done = bf16[8,64,1024]{2,1,0:T(8,128)(2,1)S(1)} async-done(((bf16[8,64,1024]{2,1,0:T(8,128)(2,1)}), bf16[8,64,1024]{2,1,0:T(8,128)(2,1)S(1)}, u32[]{:S(2)}, u32[]{:S(2)}) %all-to-all-start) | async-done | bytes 1048608 | tf_op jit(solution)/shard_map/all_to_all | solution.py:69
  35.0 3.6 %all-to-all-start.2 = ((bf16[8,64,1024]{2,1,0:T(8,128)(2,1)}), bf16[8,64,1024]{2,1,0:T(8,128)(2,1)S(1)}, u32[]{:S(2)}, u32[]{:S(2)}) async-start(bf16[8,64,1024]{2,1,0:T(8,128)(2,1)} %bitcast.11), calls=%async_computation.2 | async-start | bytes 2097152 | tf_op jit(solution)/shard_map/all_to_all | solution.py:70
  38.6 10.7 %all-gather.4.cloned.1.call-done = bf16[1,1024,768]{2,1,0:T(8,128)(2,1)} async-done(((bf16[1,256,768]{2,1,0:T(8,128)(2,1)}), bf16[1,1024,768]{2,1,0:T(8,128)(2,1)}) %all-gather.4.cloned.1.call-update) | async-done | bytes 1572880 | tf_op jit(solution)/shard_map/all_gather | solution.py:75
  49.4 3.6 %fusion.9 = f32[512,768]{1,0:T(8,128)} fusion(bf16[512,1024]{1,0:T(8,128)(2,1)S(1)} %bitcast.58, bf16[1,1024,768]{2,1,0:T(8,128)(2,1)} %all-gather.4.cloned.1.call-done), kind=kOutput, calls=%fused_computation.10 | convolution fusion | flops 805306368 | bytes 4194304 | tf_op jit(solution)/shard_map/dot_general | solution.py:10
  53.0 33.9 %all-gather.6.cloned.1.call-done = bf16[1,1024,768]{2,1,0:T(8,128)(2,1)} async-done(((bf16[1,256,768]{2,1,0:T(8,128)(2,1)}), bf16[1,1024,768]{2,1,0:T(8,128)(2,1)}) %all-gather.6.cloned.1.call-update) | async-done | bytes 1572880 | tf_op jit(solution)/shard_map/all_gather | solution.py:76
  87.0 4.0 %multiply_convert_fusion.2 = (bf16[512,768]{1,0:T(8,128)(2,1)S(1)}, f32[512,768]{1,0:T(8,128)}) fusion(f32[512,768]{1,0:T(8,128)} %fusion.9, bf16[512,1024]{1,0:T(8,128)(2,1)S(1)} %bitcast.59, bf16[1,1024,768]{2,1,0:T(8,128)(2,1)} %all-gather.6.cloned.1.call-done), kind=kOutput, calls=%fused_computation.14 | convolution fusion | flops 807665664 | bytes 6553600 | tf_op jit(solution)/shard_map/dot_general | solution.py:11
  91.0 2.7 %fusion.31 = f32[1024,768]{1,0:T(8,128)} fusion(bf16[512,1024]{1,0:T(8,128)(2,1)S(1)} %bitcast.56, bf16[512,768]{1,0:T(8,128)(2,1)S(1)} %get-tuple-element.6), kind=kOutput, calls=%fused_computation.48 | convolution fusion | flops 805306368 | bytes 4980736 | tf_op jit(solution)/shard_map/dot_general | solution.py:82
  93.7 30.8 %all-gather.8.cloned.1.call-done = bf16[1,1024,768]{2,1,0:T(8,128)(2,1)} async-done(((bf16[1,256,768]{2,1,0:T(8,128)(2,1)}), bf16[1,1024,768]{2,1,0:T(8,128)(2,1)}) %all-gather.8.cloned.1.call-update) | async-done | bytes 1572880 | tf_op jit(solution)/shard_map/all_gather | solution.py:77
  124.5 2.5 %fusion = f32[512,768]{1,0:T(8,128)S(1)} fusion(bf16[512,1024]{1,0:T(8,128)(2,1)S(1)} %bitcast.57, bf16[1,1024,768]{2,1,0:T(8,128)(2,1)} %all-gather.8.cloned.1.call-done), kind=kOutput, calls=%fused_computation.1 | convolution fusion | flops 805306368 | bytes 4194304 | tf_op jit(solution)/shard_map/dot_general | solution.py:18
  127.3 1.4 fusion.7
  128.8 2.0 %add_convert_fusion = bf16[512,1024]{1,0:T(8,128)(2,1)} fusion(f32[512,1024]{1,0:T(8,128)S(1)} %fusion.7, bf16[1,1024,768]{2,1,0:T(8,128)(2,1)S(1)} %copy-done.6, f32[512,768]{1,0:T(8,128)S(1)} %fusion, f32[512,768]{1,0:T(8,128)S(1)} %copy-done.7), kind=kOutput, calls=%fused_computation | convolution fusion | flops 808714240 | bytes 7864320 | tf_op jit(solution)/shard_map/dot_general | solution.py:26
  130.8 3.6 %all-to-all-start.3 = ((bf16[8,64,1024]{2,1,0:T(8,128)(2,1)}), bf16[8,64,1024]{2,1,0:T(8,128)(2,1)S(1)}, u32[]{:S(2)}, u32[]{:S(2)}) async-start(bf16[8,64,1024]{2,1,0:T(8,128)(2,1)} %bitcast.13), calls=%async_computation.3 | async-start | bytes 2097152 | tf_op jit(solution)/shard_map/all_to_all | solution.py:95
  134.5 3.4 %fusion.12 = bf16[512,1024]{1,0:T(8,128)(2,1)} fusion(bf16[512,768]{1,0:T(8,128)(2,1)S(1)} %get-tuple-element.6, bf16[1,1024,768]{2,1,0:T(8,128)(2,1)} %all-gather.8.cloned.1.call-done), kind=kOutput, calls=%fused_computation.17 | convolution fusion | flops 805830656 | bytes 3407872 | tf_op jit(solution)/shard_map/dot_general | solution.py:15
  137.9 12.0 %all-to-all-done.3 = bf16[8,64,1024]{2,1,0:T(8,128)(2,1)S(1)} async-done(((bf16[8,64,1024]{2,1,0:T(8,128)(2,1)}), bf16[8,64,1024]{2,1,0:T(8,128)(2,1)S(1)}, u32[]{:S(2)}, u32[]{:S(2)}) %all-to-all-start.3) | async-done | bytes 1048608 | tf_op jit(solution)/shard_map/all_to_all | solution.py:95
  149.9 3.6 %all-to-all-start.1 = ((bf16[8,64,1024]{2,1,0:T(8,128)(2,1)}), bf16[8,64,1024]{2,1,0:T(8,128)(2,1)S(1)}, u32[]{:S(2)}, u32[]{:S(2)}) async-start(bf16[8,64,1024]{2,1,0:T(8,128)(2,1)} %bitcast.8), calls=%async_computation.1 | async-start | bytes 2097152 | tf_op jit(solution)/shard_map/all_to_all | solution.py:88
  153.7 0.5 convolution_reduce_fusion
  154.2 14.6 %all-to-all-done.1 = bf16[8,64,1024]{2,1,0:T(8,128)(2,1)S(1)} async-done(((bf16[8,64,1024]{2,1,0:T(8,128)(2,1)}), bf16[8,64,1024]{2,1,0:T(8,128)(2,1)S(1)}, u32[]{:S(2)}, u32[]{:S(2)}) %all-to-all-start.1) | async-done | bytes 1048608 | tf_op jit(solution)/shard_map/all_to_all | solution.py:88
  168.8 1.1 multiply_reduce_fusion
  169.9 0.8 subtract_convert_fusion
  170.7 0.8 add_convert_fusion.1
  171.5 14.4 %reduce-scatter.2.cloned.1.call-done = f32[256,768]{1,0:T(8,128)} async-done(((f32[1024,768]{1,0:T(8,128)}), f32[256,768]{1,0:T(8,128)}) %reduce-scatter.2.cloned.1.call-update) | async-done | bytes 786448 | tf_op jit(solution)/shard_map/reduce_scatter | solution.py:85
  185.8 2.1 %multiply_bitcast_fusion = f32[1,256,768]{2,1,0:T(8,128)} fusion(f32[256,768]{1,0:T(8,128)} %reduce-scatter.2.cloned.1.call-done), kind=kLoop, calls=%fused_computation.24 | loop fusion | flops 196608 | bytes 1572864 | tf_op jit(solution)/shard_map/broadcast_in_dim | solution.py:86
  (40 shorter events, 2.1 us)
Async XLA Ops:
  7.2 42.2 %all-gather.4.cloned.1.call-start = ((), (), s32[]{:S(2)}) async-start(), calls=%async_computation.5 | async-start | bytes 1966080 | tf_op jit(solution)/shard_map/all_gather | solution.py:75
  7.9 79.1 %all-gather.6.cloned.1.call-start = ((), (), s32[]{:S(2)}) async-start(), calls=%async_computation.6 | async-start | bytes 1966080 | tf_op jit(solution)/shard_map/all_gather | solution.py:76
  8.6 115.9 %all-gather.8.cloned.1.call-start = ((), (), s32[]{:S(2)}) async-start(), calls=%async_computation.7 | async-start | bytes 1966080 | tf_op jit(solution)/shard_map/all_gather | solution.py:77
  12.9 6.8 %copy-start = (bf16[128,1024]{1,0:T(8,128)(2,1)S(1)}, bf16[128,1024]{1,0:T(8,128)(2,1)}, u32[]{:S(2)}) copy-start(bf16[128,1024]{1,0:T(8,128)(2,1)} %param.12) | copy-start | bytes 786436
  14.5 20.6 %all-to-all-start = ((bf16[8,64,1024]{2,1,0:T(8,128)(2,1)}), bf16[8,64,1024]{2,1,0:T(8,128)(2,1)S(1)}, u32[]{:S(2)}, u32[]{:S(2)}) async-start(bf16[8,64,1024]{2,1,0:T(8,128)(2,1)} %bitcast.3), calls=%async_computation | async-start | bytes 2097152 | tf_op jit(solution)/shard_map/all_to_all | solution.py:69
  19.6 1.0 copy-start.4
  35.0 56.0 %all-to-all-start.2 = ((bf16[8,64,1024]{2,1,0:T(8,128)(2,1)}), bf16[8,64,1024]{2,1,0:T(8,128)(2,1)S(1)}, u32[]{:S(2)}, u32[]{:S(2)}) async-start(bf16[8,64,1024]{2,1,0:T(8,128)(2,1)} %bitcast.11), calls=%async_computation.2 | async-start | bytes 2097152 | tf_op jit(solution)/shard_map/all_to_all | solution.py:70
  38.6 147.2 %reduce-scatter.2.cloned.1.call-start = ((), (), s32[]{:S(2)}) async-start(), calls=%async_computation.8 | async-start | bytes 3932160 | tf_op jit(solution)/shard_map/reduce_scatter | solution.py:85
  124.5 2.5 %copy-start.5 = (bf16[1,1024,768]{2,1,0:T(8,128)(2,1)S(1)}, bf16[1,1024,768]{2,1,0:T(8,128)(2,1)}, u32[]{:S(2)}) copy-start(bf16[1,1024,768]{2,1,0:T(8,128)(2,1)} %all-gather.4.cloned.1.call-done) | copy-start | bytes 4718596
  124.5 2.6 %copy-start.7 = (f32[512,768]{1,0:T(8,128)S(1)}, f32[512,768]{1,0:T(8,128)}, u32[]{:S(2)}) copy-start(f32[512,768]{1,0:T(8,128)} %fusion.9) | copy-start | bytes 4718596
  124.5 2.8 %copy-start.8 = (f32[512,768]{1,0:T(8,128)S(1)}, f32[512,768]{1,0:T(8,128)}, u32[]{:S(2)}) copy-start(f32[512,768]{1,0:T(8,128)} %get-tuple-element.7) | copy-start | bytes 4718596
  127.3 1.4 copy-start.6
  130.8 19.0 %all-to-all-start.3 = ((bf16[8,64,1024]{2,1,0:T(8,128)(2,1)}), bf16[8,64,1024]{2,1,0:T(8,128)(2,1)S(1)}, u32[]{:S(2)}, u32[]{:S(2)}) async-start(bf16[8,64,1024]{2,1,0:T(8,128)(2,1)} %bitcast.13), calls=%async_computation.3 | async-start | bytes 2097152 | tf_op jit(solution)/shard_map/all_to_all | solution.py:95
  137.9 15.8 %copy-start.3 = (s32[128,2]{0,1:T(2,128)S(1)}, s32[128,2]{0,1:T(2,128)}, u32[]{:S(2)}) copy-start(s32[128,2]{0,1:T(2,128)} %param.13) | copy-start | bytes 3076
  149.9 18.9 %all-to-all-start.1 = ((bf16[8,64,1024]{2,1,0:T(8,128)(2,1)}), bf16[8,64,1024]{2,1,0:T(8,128)(2,1)S(1)}, u32[]{:S(2)}, u32[]{:S(2)}) async-start(bf16[8,64,1024]{2,1,0:T(8,128)(2,1)} %bitcast.8), calls=%async_computation.1 | async-start | bytes 2097152 | tf_op jit(solution)/shard_map/all_to_all | solution.py:88
  154.2 15.7 %copy-start.1 = (bf16[128,1024]{1,0:T(8,128)(2,1)S(1)}, bf16[128,1024]{1,0:T(8,128)(2,1)}, u32[]{:S(2)}) copy-start(bf16[128,1024]{1,0:T(8,128)(2,1)} %param.10) | copy-start | bytes 786436
  168.8 1.9 copy-start.2
Sparse Core Ops, SparseCore 0:
  9.6 39.7 all-gather.3
  51.0 35.9 all-gather.5
  88.5 35.9 all-gather.7
  126.7 59.1 reduce-scatter.1
where the time goes:
time: 195 us; the launch traced here: 194 us
  waiting for transfers between devices  131 us (67%)
  matrix products  24.5 us (13%)
  starting transfers between devices  16.1 us (8%)
  between operations  13.9 us (7%)
  local copies, waits for them, and re-layouts  4.45 us (2%)
  other arithmetic  4.37 us (2%)
    all_gather x1, waiting for transfers between devices, per_device(): lax.all_gather(w_up, 'dp', axis=1, tiled=True)  33.9 us
    all_gather x1, waiting for transfers between devices, per_device(): lax.all_gather(w_down, 'dp', axis=1, tiled=True)  30.8 us
    all_to_all x1, waiting for transfers between devices, per_device(): lax.all_to_all(out_rows.reshape(owners, capacity, feature_count), 'expert...  14.6 us
    reduce_scatter x1, waiting for transfers between devices, per_device(): lax.psum_scatter(partial_grad, 'dp', scatter_dimension=0, tiled=True)  14.4 us
    all_to_all x1, waiting for transfers between devices, per_device(): lax.all_to_all(send_input, 'expert', split_axis=0, concat_axis=0, tiled=T...  12.6 us
    all_to_all x1, waiting for transfers between devices, per_device(): lax.all_to_all(input_cot.reshape(owners, capacity, feature_count), 'exper...  12 us
    all_gather x1, waiting for transfers between devices, per_device(): lax.all_gather(w_gate, 'dp', axis=1, tiled=True)  10.7 us
    all_to_all x1, starting transfers between devices, per_device(): lax.all_to_all(send_input, 'expert', split_axis=0, concat_axis=0, tiled=T...  5.17 us
  transfers between devices with their start and end apart: 8, of which 7 were waited for; matrix products, arithmetic and copies ran while one was open for 16% of the time, Pallas kernels for 0%

commit v1 on v0

v1 whole, which is shorter than its diff:
```python
import functools
import math

import jax
import jax.numpy as jnp
from jax import lax
from jax.experimental import pallas as pl
from jax.experimental.pallas import tpu as pltpu
from jax.sharding import PartitionSpec as P

BF = jnp.bfloat16
F32 = jnp.float32
MESH = pl.DeviceIdType.MESH


def mm(a, b, ca, cb):
    return lax.dot_general(a, b, (((ca,), (cb,)), ((), ())), preferred_element_type=F32)


def tiles(extent, size=256):
    size = min(size, extent)
    return [slice(at, at + size) for at in range(0, extent, size)]


def layer_kernel(
    n, owners, cap, scale,
    x_ref, so_ref, fg_ref, sg_ref, routes_ref, gv_ref, wg_hbm, wu_hbm, wd_hbm,
    si_ref, ft_ref, gg_ref, wdg_ref,
    wbuf, s_in, s_cot, r_in, r_cot, hid, act, fac, gc, uc,
    o_out, b_out, o_cot, b_cot, part, rs_send, rs_recv, qbuf,
    lsem, wss, wrs, ass, ars, oss, ors, css, crs, rss, rrs,
):
    z = lax.axis_index("dp")
    me = lax.axis_index("expert")
    count, width = x_ref.shape
    top = routes_ref.shape[1]
    slots = owners * cap
    depth, units = wbuf.shape[2], wbuf.shape[3]

    def peers(body):
        def step(o, carry):
            body(o, lax.rem(me + o, owners))
            return carry
        lax.fori_loop(1, owners, step, 0)

    barrier = pltpu.get_barrier_semaphore()
    peers(lambda o, to: pl.semaphore_signal(
        barrier, inc=1, device_id={"expert": to}, device_id_type=MESH))

    @pl.when(z > 0)
    def _():
        pl.semaphore_signal(barrier, inc=1, device_id={"dp": z - 1}, device_id_type=MESH)

    @pl.when(z < n - 1)
    def _():
        pl.semaphore_signal(barrier, inc=1, device_id={"dp": z + 1}, device_id_type=MESH)

    local = [
        pltpu.make_async_copy(w.at[0], wbuf.at[m, z], lsem.at[m])
        for m, w in enumerate((wg_hbm, wu_hbm, wd_hbm))
    ]
    for copy in local:
        copy.start()

    routes = routes_ref[...]
    gates = gv_ref[...]
    ids = lax.broadcasted_iota(jnp.int32, (count, owners), 1)
    lower = (
        lax.broadcasted_iota(jnp.int32, (count, count), 1)
        < lax.broadcasted_iota(jnp.int32, (count, count), 0)
    ).astype(F32).astype(BF)
    slot_ids = lax.broadcasted_iota(jnp.int32, (count, slots), 1)
    base = jnp.zeros((1, owners), F32)
    for k in range(top):
        onehot = (routes[:, k:k + 1] == ids).astype(F32)
        before = mm(lower, onehot.astype(BF), 1, 0) + base
        place = jnp.sum(onehot * (before + ids.astype(F32) * cap), axis=1, keepdims=True)
        base = base + jnp.sum(onehot, axis=0, keepdims=True)
        qbuf[k] = (place.astype(jnp.int32) == slot_ids).astype(F32).astype(BF)

    def wcopy(m, s, way, shard, to):
        return pltpu.make_async_remote_copy(
            src_ref=wbuf.at[m, shard], dst_ref=wbuf.at[m, shard],
            send_sem=wss.at[way, m, s], recv_sem=wrs.at[way, m, s],
            device_id={"dp": to}, device_id_type=MESH)

    def wsend(m, s, finish=False):
        @pl.when((z >= s) & (z < n - 1))
        def _():
            copy = wcopy(m, s, 0, z - s, z + 1)
            copy.wait_send() if finish else copy.start()

        @pl.when((z + s <= n - 1) & (z > 0))
        def _():
            copy = wcopy(m, s, 1, z + s, z - 1)
            copy.wait_send() if finish else copy.start()

    def wrecv(m, s):
        @pl.when(z - 1 - s >= 0)
        def _():
            wcopy(m, s, 0, z - 1 - s, z - 1).wait_recv()

        @pl.when(z + 1 + s <= n - 1)
        def _():
            wcopy(m, s, 1, z + 1 + s, z + 1).wait_recv()

    for copy in local:
        copy.wait()
    pl.semaphore_wait(barrier, owners - 1 + jnp.minimum(z, 1) + jnp.minimum(n - 1 - z, 1))

    wsend(0, 0)
    wsend(1, 0)

    def acopy(a, o, to):
        src, dst = ((s_in, r_in), (s_cot, r_cot))[a]
        return pltpu.make_async_remote_copy(
            src_ref=src.at[to], dst_ref=dst.at[me],
            send_sem=ass.at[a, o], recv_sem=ars.at[a, o],
            device_id={"expert": to}, device_id_type=MESH)

    both = sum(qbuf[k].astype(F32) for k in range(top)).astype(BF)
    for c in tiles(width):
        rows = mm(both, x_ref[:, c], 0, 0).astype(BF)
        s_in[:, :, c] = rows.reshape(owners, cap, rows.shape[1])
    peers(lambda o, to: acopy(0, o, to).start())
    r_in[me] = s_in[me]
    for c in tiles(width):
        grads = sg_ref[:, c].astype(F32)
        rows = sum(
            mm(qbuf[k], (gates[:, k:k + 1] * grads).astype(BF), 0, 0) for k in range(top)
        ).astype(BF)
        s_cot[:, :, c] = rows.reshape(owners, cap, rows.shape[1])
    peers(lambda o, to: acopy(1, o, to).start())
    r_cot[me] = s_cot[me]

    for s in range(n - 1):
        for m in (0, 1):
            wrecv(m, s)
            if s + 1 < n - 1:
                wsend(m, s + 1)
        if s == max(n - 3, 0):
            wsend(2, 0)
    peers(lambda o, to: acopy(0, o, to).wait_recv())
    peers(lambda o, to: acopy(1, o, to).wait_recv())

    rows_in = r_in[...].reshape(slots, width)
    for c in tiles(units):
        size = c.stop - c.start
        pre_gate = mm(rows_in, wbuf[0, :, :, c].reshape(width, size), 1, 0)
        pre_up = mm(rows_in, wbuf[1, :, :, c].reshape(width, size), 1, 0)
        squashed = jax.nn.sigmoid(pre_gate)
        activated = pre_gate * squashed
        hid[:, c] = (activated * pre_up).astype(BF)
        act[:, c] = activated
        fac[:, c] = pre_up * squashed * (1.0 + pre_gate * (1.0 - squashed))

    def ocopy(j, o, to):
        return pltpu.make_async_remote_copy(
            src_ref=o_out.at[j, to], dst_ref=b_out.at[j, me],
            send_sem=oss.at[j, o], recv_sem=ors.at[j, o],
            device_id={"expert": to}, device_id_type=MESH)

    def out_shard(j):
        rows = mm(hid[...], wbuf[2, j], 1, 1).astype(BF)
        o_out[j] = rows.reshape(owners, cap, depth)
        peers(lambda o, to: ocopy(j, o, to).start())
        b_out[j, me] = o_out[j, me]

    out_shard(z)

    for c in tiles(width):
        part[c, :] = mm(r_cot[:, :, c].reshape(slots, c.stop - c.start), hid[...], 0, 0)

    def rcopy(way, j, to):
        return pltpu.make_async_remote_copy(
            src_ref=rs_send.at[j], dst_ref=rs_recv.at[way, j],
            send_sem=rss.at[way, j], recv_sem=rrs.at[way, j],
            device_id={"dp": to}, device_id_type=MESH)

    def rstep(way, j):
        behind = z - 1 if way == 0 else z + 1
        ahead = z + 1 if way == 0 else z - 1
        first = z == 0 if way == 0 else z == n - 1
        mine = part[j * depth:(j + 1) * depth, :]

        @pl.when(z < j if way == 0 else z > j)
        def _():
            @pl.when(first)
            def _():
                rs_send[j] = mine.astype(BF)

            @pl.when(jnp.logical_not(first))
            def _():
                rcopy(way, j, behind).wait_recv()
                rs_send[j] = (mine + rs_recv[way, j].astype(F32)).astype(BF)

            rcopy(way, j, ahead).start()

    for s in range(n - 1):
        wrecv(2, s)
        if s + 1 < n - 1:
            wsend(2, s + 1)
        rstep(0, n - 1 - s)
        rstep(1, s)

        @pl.when(z - 1 - s >= 0)
        def _():
            out_shard(z - 1 - s)

        @pl.when(z + 1 + s <= n - 1)
        def _():
            out_shard(z + 1 + s)

    rows_cot = r_cot[...].reshape(slots, width)
    for c in tiles(units):
        hidden_cot = mm(rows_cot, wbuf[2, :, :, c].reshape(width, c.stop - c.start), 1, 0)
        gc[:, c] = (hidden_cot * fac[:, c]).astype(BF)
        uc[:, c] = (hidden_cot * act[:, c]).astype(BF)

    def ccopy(j, o, to):
        return pltpu.make_async_remote_copy(
            src_ref=o_cot.at[j, to], dst_ref=b_cot.at[j, me],
            send_sem=css.at[j, o], recv_sem=crs.at[j, o],
            device_id={"expert": to}, device_id_type=MESH)

    def cot_shard(j, carry):
        rows = mm(gc[...], wbuf[0, j], 1, 1) + mm(uc[...], wbuf[1, j], 1, 1)
        o_cot[j] = rows.astype(BF).reshape(owners, cap, depth)
        peers(lambda o, to: ccopy(j, o, to).start())
        b_cot[j, me] = o_cot[j, me]
        return carry

    lax.fori_loop(0, n, cot_shard, 0)

    sums = [jnp.zeros((count, 1), F32) for _ in range(top)]
    for j in range(n):
        c = slice(j * depth, (j + 1) * depth)
        peers(lambda o, to: ocopy(j, o, to).wait_recv())
        rows = b_out[j].reshape(slots, depth)
        combined = jnp.zeros((count, depth), F32)
        grads = sg_ref[:, c].astype(F32)
        for k in range(top):
            chosen = mm(qbuf[k], rows, 1, 0)
            combined = combined + gates[:, k:k + 1] * chosen
            sums[k] = sums[k] + jnp.sum(grads * chosen, axis=1, keepdims=True)
        si_ref[:, c] = (so_ref[:, c].astype(F32) - combined).astype(BF)
    for k in range(top):
        gg_ref[:, k:k + 1] = sums[k]

    own = pl.ds(pl.multiple_of(z * depth, depth), depth)

    @pl.when(z > 0)
    def _():
        rcopy(0, z, z - 1).wait_recv()
        part[own, :] = part[own, :] + rs_recv[0, z].astype(F32)

    @pl.when(z < n - 1)
    def _():
        rcopy(1, z, z + 1).wait_recv()
        part[own, :] = part[own, :] + rs_recv[1, z].astype(F32)

    wdg_ref[0] = part[own, :] * scale

    both = sum(qbuf[k].astype(F32) for k in range(top)).astype(BF)
    for j in range(n):
        c = slice(j * depth, (j + 1) * depth)
        peers(lambda o, to: ccopy(j, o, to).wait_recv())
        total = mm(both, b_cot[j].reshape(slots, depth), 1, 0)
        ft_ref[:, c] = (fg_ref[:, c].astype(F32) + total).astype(BF)

    for s in range(n - 1):
        for m in (0, 1, 2):
            wsend(m, s, finish=True)

        @pl.when(z < n - 1 - s)
        def _():
            rcopy(0, n - 1 - s, z + 1).wait_send()

        @pl.when(z > s)
        def _():
            rcopy(1, s, z - 1).wait_send()

    for a in (0, 1):
        peers(lambda o, to: acopy(a, o, to).wait_send())

    def sent(j, carry):
        peers(lambda o, to: ocopy(j, o, to).wait_send())
        peers(lambda o, to: ccopy(j, o, to).wait_send())
        return carry

    lax.fori_loop(0, n, sent, 0)


def per_device(
    first_out, second_out, first_grad, second_grad, routes, gate_values, w_gate, w_up, w_down
):
    count, width = first_out.shape
    top = routes.shape[1]
    owners = lax.axis_size("expert")
    n = lax.axis_size("dp")
    cap = min(count, 2 * count * top // owners)
    slots = owners * cap
    depth, units = w_gate.shape[1:]
    vmem = pl.BlockSpec(memory_space=pltpu.VMEM)
    hbm = pl.BlockSpec(memory_space=pl.ANY)
    dma = pltpu.SemaphoreType.DMA
    rows = pltpu.VMEM((owners, cap, width), BF)
    shards = pltpu.VMEM((n, owners, cap, depth), BF)
    return pl.pallas_call(
        functools.partial(layer_kernel, n, owners, cap, 1.0 / math.sqrt(count * n)),
        out_shape=(
            jax.ShapeDtypeStruct((count, width), BF),
            jax.ShapeDtypeStruct((count, width), BF),
            jax.ShapeDtypeStruct((count, top), F32),
            jax.ShapeDtypeStruct((1, depth, units), F32),
        ),
        in_specs=[vmem] * 6 + [hbm] * 3,
        out_specs=(vmem,) * 4,
        scratch_shapes=[
            pltpu.VMEM((3, n, depth, units), BF),
            rows, rows, rows, rows,
            pltpu.VMEM((slots, units), BF),
            pltpu.VMEM((slots, units), F32),
            pltpu.VMEM((slots, units), F32),
            pltpu.VMEM((slots, units), BF),
            pltpu.VMEM((slots, units), BF),
            shards, shards, shards, shards,
            pltpu.VMEM((width, units), F32),
            pltpu.VMEM((n, depth, units), BF),
            pltpu.VMEM((2, n, depth, units), BF),
            pltpu.VMEM((top, count, slots), BF),
            dma((3,)),
            dma((2, 3, n - 1)), dma((2, 3, n - 1)),
            dma((2, owners)), dma((2, owners)),
            dma((n, owners)), dma((n, owners)),
            dma((n, owners)), dma((n, owners)),
            dma((2, n)), dma((2, n)),
        ],
        compiler_params=pltpu.CompilerParams(
            collective_id=0, has_side_effects=True, vmem_limit_bytes=56 * 1024 * 1024
        ),
    )(first_out, second_out, first_grad, second_grad, routes, gate_values, w_gate, w_up, w_down)


def solution(mesh):
    rows = P(("dp", "expert"), None)
    mats = P("expert", "dp", None)
    return jax.shard_map(
        per_device,
        mesh=mesh,
        in_specs=(rows,) * 6 + (mats,) * 3,
        out_specs=(rows, rows, rows, mats),
        check_vma=False,
    )
```

time: 195 us -> 132 us (0.68)
  waiting for transfers between devices: 131 us -> 0 us
  Pallas kernels: 0 us -> 123 us
  matrix products: 24.5 us -> 0 us
  starting transfers between devices: 16.1 us -> 0 us
  between operations: 13.9 us -> 0.66 us
  other arithmetic: 4.37 us -> 0 us
  local copies, waits for them, and re-layouts: 4.45 us -> 7.93 us
    pallas_call x0 -> x1, Pallas kernels: none -> 123 us  [per_device(): pl.pallas_call(functools.partial(layer_kernel, n, owners, cap, 1.0 / math...]
    all_gather x3 -> x0, waiting for transfers between devices: 75.5 us -> none  [the longest x1 33.9 us: per_device(): lax.all_gather(w_up, 'dp', axis=1, tiled=True)]
    all_to_all x4 -> x0, waiting for transfers between devices: 39.1 us -> none  [the longest x1 14.6 us: per_device(): lax.all_to_all(out_rows.reshape(owners, capacity, feature_count), 'expert...]
    dot_general x11 -> x0, matrix products: 24.5 us -> none  [the longest x1 4.03 us: expert_rows(): pre_up = jnp.dot(rows_in, up_mat, preferred_element_type=jnp.float32)]
    all_to_all x4 -> x0, starting transfers between devices: 15.9 us -> none  [the longest x1 5.17 us: per_device(): lax.all_to_all(send_input, 'expert', split_axis=0, concat_axis=0, tiled=T...]
    reduce_scatter x1 -> x0, waiting for transfers between devices: 14.4 us -> none  [per_device(): lax.psum_scatter(partial_grad, 'dp', scatter_dimension=0, tiled=True)]
    unnamed x20 -> x9, local copies, waits for them, and re-layouts: 1.2 us -> 6.38 us
    broadcast_in_dim x1 -> x0, other arithmetic: 2.08 us -> none  [per_device(): w_down_grad = (reduced * grad_scale)[None]]
  transfers between devices with their start and end apart: 8 -> 0, of which waited for: 7 -> 0; matrix products, arithmetic and copies ran while one was open for 16% -> 0% of each run, Pallas kernels for 0% -> 0%
where the time goes in v1:
time: 132 us; the launch traced here: 131 us
  Pallas kernels  123 us (93%)
  local copies, waits for them, and re-layouts  7.93 us (6%)
    pallas_call x1, Pallas kernels, per_device(): pl.pallas_call(functools.partial(layer_kernel, n, owners, cap, 1.0 / math...  123 us
    unnamed x9, local copies, waits for them, and re-layouts  6.38 us

profile of v1, /device:TPU:0, one launch (start us, length us, event | category | flops | bytes accessed | tf_op | source)
XLA Modules:
  0.0 131.4 jit_solution(13310118250848519492)
XLA Ops:
  0.6 0.0 copy-start.1
  0.6 1.4 %copy.13.routes_ref = s32[128,2]{1,0:T(8,128)} copy(s32[128,2]{0,1:T(2,128)} %param.13) | data formatting | bytes 2048 | tf_op args[4]
  2.1 0.0 copy-done.1
  2.1 0.7 copy.14.gv_ref
  2.8 122.9 %shard_map.120 = (bf16[128,1024]{1,0:T(8,128)(2,1)}, bf16[128,1024]{1,0:T(8,128)(2,1)}, f32[128,2]{1,0:T(8,128)}, f32[1,256,768]{2,1,0:T(8,128)}) custom-call(bf16[128,1024]{1,0:T(8,128)(2,1)} %x_ref.1, bf16[128,1024]{1,0:T(8,128)(2,1)} %so_ref.1, bf16[128,1024]{1,0:T(8,128)(2,1)} %fg_ref.1, bf16[128,1024]{1,0:T(8,128)(2,1)} %sg_ref.1, ...), custom_call_target="tpu_custom_call" | custom-call | tf_op jit(solution)/shard_map/pallas_call | solution.py:309
  125.7 0.0 copy-start
  125.7 1.5 %copy.15 = f32[128,2]{0,1:T(2,128)} copy(f32[128,2]{1,0:T(8,128)} %get-tuple-element.6) | data formatting | bytes 2048 | tf_op jit(solution)/shard_map/pallas_call | solution.py:309
  127.2 1.7 %copy.19 = bf16[128,1024]{1,0:T(8,128)(2,1)} copy(bf16[128,1024]{1,0:T(8,128)(2,1)} %get-tuple-element.12) | data formatting | bytes 524288
  128.9 1.7 %copy.20 = bf16[128,1024]{1,0:T(8,128)(2,1)} copy(bf16[128,1024]{1,0:T(8,128)(2,1)} %get-tuple-element.13) | data formatting | bytes 524288
  130.6 0.0 copy-done
  130.6 0.9 copy.21
Async XLA Ops:
  0.6 1.4 %copy-start.1 = (f32[128,2]{0,1:T(2,128)S(1)}, f32[128,2]{0,1:T(2,128)}, u32[]{:S(2)}) copy-start(f32[128,2]{0,1:T(2,128)} %param.14) | copy-start | bytes 3076
  125.7 4.9 %copy-start = (f32[1,256,768]{2,1,0:T(8,128)S(1)}, f32[1,256,768]{2,1,0:T(8,128)}, u32[]{:S(2)}) copy-start(f32[1,256,768]{2,1,0:T(8,128)} %get-tuple-element.15) | copy-start | bytes 2359300

commit v2 on v1

--- a/solution.py
+++ b/solution.py
@@ -33,7 +33,7 @@
     z = lax.axis_index("dp")
     me = lax.axis_index("expert")
     count, width = x_ref.shape
-    top = routes_ref.shape[1]
+    top = routes_ref.shape[0]
     slots = owners * cap
     depth, units = wbuf.shape[2], wbuf.shape[3]
 
@@ -46,14 +46,9 @@
     barrier = pltpu.get_barrier_semaphore()
     peers(lambda o, to: pl.semaphore_signal(
         barrier, inc=1, device_id={"expert": to}, device_id_type=MESH))
-
-    @pl.when(z > 0)
-    def _():
-        pl.semaphore_signal(barrier, inc=1, device_id={"dp": z - 1}, device_id_type=MESH)
-
-    @pl.when(z < n - 1)
-    def _():
-        pl.semaphore_signal(barrier, inc=1, device_id={"dp": z + 1}, device_id_type=MESH)
+    for s in range(1, n):
+        pl.semaphore_signal(
+            barrier, inc=1, device_id={"dp": lax.rem(z + s, n)}, device_id_type=MESH)
 
     local = [
         pltpu.make_async_copy(w.at[0], wbuf.at[m, z], lsem.at[m])
@@ -62,8 +57,19 @@
     for copy in local:
         copy.start()
 
-    routes = routes_ref[...]
-    gates = gv_ref[...]
+    eye = (
+        lax.broadcasted_iota(jnp.int32, (count, count), 0)
+        == lax.broadcasted_iota(jnp.int32, (count, count), 1)
+    )
+
+    def column(row):
+        return jnp.sum(jnp.where(eye, row, jnp.zeros_like(row)), axis=1, keepdims=True)
+
+    def as_row(col):
+        return jnp.sum(jnp.where(eye, col, jnp.zeros_like(col)), axis=0, keepdims=True)
+
+    routes = [column(routes_ref[k:k + 1, :]) for k in range(top)]
+    gates = [column(gv_ref[k:k + 1, :]) for k in range(top)]
     ids = lax.broadcasted_iota(jnp.int32, (count, owners), 1)
     lower = (
         lax.broadcasted_iota(jnp.int32, (count, count), 1)
@@ -72,7 +78,7 @@
     slot_ids = lax.broadcasted_iota(jnp.int32, (count, slots), 1)
     base = jnp.zeros((1, owners), F32)
     for k in range(top):
-        onehot = (routes[:, k:k + 1] == ids).astype(F32)
+        onehot = (routes[k] == ids).astype(F32)
         before = mm(lower, onehot.astype(BF), 1, 0) + base
         place = jnp.sum(onehot * (before + ids.astype(F32) * cap), axis=1, keepdims=True)
         base = base + jnp.sum(onehot, axis=0, keepdims=True)
@@ -104,9 +110,21 @@
         def _():
             wcopy(m, s, 1, z + 1 + s, z + 1).wait_recv()
 
+    def dsend(finish=False):
+        for s in reversed(range(n - 1)):
+            @pl.when(z + 1 + s <= n - 1)
+            def _():
+                copy = wcopy(2, s, 0, z, z + 1 + s)
+                copy.wait_send() if finish else copy.start()
+
+            @pl.when(z - 1 - s >= 0)
+            def _():
+                copy = wcopy(2, s, 1, z, z - 1 - s)
+                copy.wait_send() if finish else copy.start()
+
     for copy in local:
         copy.wait()
-    pl.semaphore_wait(barrier, owners - 1 + jnp.minimum(z, 1) + jnp.minimum(n - 1 - z, 1))
+    pl.semaphore_wait(barrier, owners + n - 2)
 
     wsend(0, 0)
     wsend(1, 0)
@@ -127,7 +145,7 @@
     for c in tiles(width):
         grads = sg_ref[:, c].astype(F32)
         rows = sum(
-            mm(qbuf[k], (gates[:, k:k + 1] * grads).astype(BF), 0, 0) for k in range(top)
+            mm(qbuf[k], (gates[k] * grads).astype(BF), 0, 0) for k in range(top)
         ).astype(BF)
         s_cot[:, :, c] = rows.reshape(owners, cap, rows.shape[1])
     peers(lambda o, to: acopy(1, o, to).start())
@@ -139,7 +157,7 @@
             if s + 1 < n - 1:
                 wsend(m, s + 1)
         if s == max(n - 3, 0):
-            wsend(2, 0)
+            dsend()
     peers(lambda o, to: acopy(0, o, to).wait_recv())
     peers(lambda o, to: acopy(1, o, to).wait_recv())
 
@@ -177,31 +195,31 @@
             send_sem=rss.at[way, j], recv_sem=rrs.at[way, j],
             device_id={"dp": to}, device_id_type=MESH)
 
+    def rfirst(way, j):
+        ahead = z + 1 if way == 0 else z - 1
+
+        @pl.when((z == 0) & (z < j) if way == 0 else (z == n - 1) & (z > j))
+        def _():
+            rs_send[j] = part[j * depth:(j + 1) * depth, :].astype(BF)
+            rcopy(way, j, ahead).start()
+
     def rstep(way, j):
         behind = z - 1 if way == 0 else z + 1
         ahead = z + 1 if way == 0 else z - 1
-        first = z == 0 if way == 0 else z == n - 1
-        mine = part[j * depth:(j + 1) * depth, :]
-
-        @pl.when(z < j if way == 0 else z > j)
-        def _():
-            @pl.when(first)
-            def _():
-                rs_send[j] = mine.astype(BF)
-
-            @pl.when(jnp.logical_not(first))
-            def _():
-                rcopy(way, j, behind).wait_recv()
-                rs_send[j] = (mine + rs_recv[way, j].astype(F32)).astype(BF)
-
+
+        @pl.when((z > 0) & (z < j) if way == 0 else (z < n - 1) & (z > j))
+        def _():
+            rcopy(way, j, behind).wait_recv()
+            mine = part[j * depth:(j + 1) * depth, :]
+            rs_send[j] = (mine + rs_recv[way, j].astype(F32)).astype(BF)
             rcopy(way, j, ahead).start()
+
+    for s in range(n - 1):
+        rfirst(0, n - 1 - s)
+        rfirst(1, s)
 
     for s in range(n - 1):
         wrecv(2, s)
-        if s + 1 < n - 1:
-            wsend(2, s + 1)
-        rstep(0, n - 1 - s)
-        rstep(1, s)
 
         @pl.when(z - 1 - s >= 0)
         def _():
@@ -210,6 +228,10 @@
         @pl.when(z + 1 + s <= n - 1)
         def _():
             out_shard(z + 1 + s)
+
+        if s < n - 2:
+            rstep(0, n - 1 - s)
+            rstep(1, s)
 
     rows_cot = r_cot[...].reshape(slots, width)
     for c in tiles(units):
@@ -241,11 +263,11 @@
         grads = sg_ref[:, c].astype(F32)
         for k in range(top):
             chosen = mm(qbuf[k], rows, 1, 0)
-            combined = combined + gates[:, k:k + 1] * chosen
+            combined = combined + gates[k] * chosen
             sums[k] = sums[k] + jnp.sum(grads * chosen, axis=1, keepdims=True)
         si_ref[:, c] = (so_ref[:, c].astype(F32) - combined).astype(BF)
     for k in range(top):
-        gg_ref[:, k:k + 1] = sums[k]
+        gg_ref[k:k + 1, :] = as_row(sums[k])
 
     own = pl.ds(pl.multiple_of(z * depth, depth), depth)
 
@@ -268,8 +290,9 @@
         total = mm(both, b_cot[j].reshape(slots, depth), 1, 0)
         ft_ref[:, c] = (fg_ref[:, c].astype(F32) + total).astype(BF)
 
+    dsend(finish=True)
     for s in range(n - 1):
-        for m in (0, 1, 2):
+        for m in (0, 1):
             wsend(m, s, finish=True)
 
         @pl.when(z < n - 1 - s)
@@ -306,12 +329,12 @@
     dma = pltpu.SemaphoreType.DMA
     rows = pltpu.VMEM((owners, cap, width), BF)
     shards = pltpu.VMEM((n, owners, cap, depth), BF)
-    return pl.pallas_call(
+    second_in, first_total, gate_grad, down_grad = pl.pallas_call(
         functools.partial(layer_kernel, n, owners, cap, 1.0 / math.sqrt(count * n)),
         out_shape=(
             jax.ShapeDtypeStruct((count, width), BF),
             jax.ShapeDtypeStruct((count, width), BF),
-            jax.ShapeDtypeStruct((count, top), F32),
+            jax.ShapeDtypeStruct((top, count), F32),
             jax.ShapeDtypeStruct((1, depth, units), F32),
         ),
         in_specs=[vmem] * 6 + [hbm] * 3,
@@ -339,7 +362,11 @@
         compiler_params=pltpu.CompilerParams(
             collective_id=0, has_side_effects=True, vmem_limit_bytes=56 * 1024 * 1024
         ),
-    )(first_out, second_out, first_grad, second_grad, routes, gate_values, w_gate, w_up, w_down)
+    )(
+        first_out, second_out, first_grad, second_grad, routes.T, gate_values.T,
+        w_gate, w_up, w_down,
+    )
+    return (second_in, first_total, gate_grad.T, down_grad)
 
 
 def solution(mesh):

time: 132 us -> 125 us (0.947)
  Pallas kernels: 123 us -> 119 us
  local copies, waits for them, and re-layouts: 7.93 us -> 4.86 us
    pallas_call x1, Pallas kernels: 123 us -> 119 us  [per_device(): pl.pallas_call(functools.partial(layer_kernel, n, owners, cap, 1.0 / math...]
    pallas_call x1 -> x0, local copies, waits for them, and re-layouts: 1.55 us -> none  [per_device(): pl.pallas_call(functools.partial(layer_kernel, n, owners, cap, 1.0 / math...]
    unnamed x9 -> x8, local copies, waits for them, and re-layouts: 6.38 us -> 4.86 us
where the time goes in v2:
time: 125 us; the launch traced here: 124 us
  Pallas kernels  119 us (95%)
  local copies, waits for them, and re-layouts  4.86 us (4%)
    pallas_call x1, Pallas kernels, per_device(): pl.pallas_call(functools.partial(layer_kernel, n, owners, cap, 1.0 / math...  119 us
    unnamed x8, local copies, waits for them, and re-layouts  4.86 us

profile of v2, /device:TPU:0, one launch (start us, length us, event | category | flops | bytes accessed | tf_op | source)
XLA Modules:
  0.0 124.5 jit_solution(13622585729515583398)
XLA Ops:
  0.6 119.0 %shard_map.120 = (bf16[128,1024]{1,0:T(8,128)(2,1)}, bf16[128,1024]{1,0:T(8,128)(2,1)}, f32[2,128]{1,0:T(2,128)}, f32[1,256,768]{2,1,0:T(8,128)}) custom-call(bf16[128,1024]{1,0:T(8,128)(2,1)} %x_ref.1, bf16[128,1024]{1,0:T(8,128)(2,1)} %so_ref.1, bf16[128,1024]{1,0:T(8,128)(2,1)} %fg_ref.1, bf16[128,1024]{1,0:T(8,128)(2,1)} %sg_ref.1, s32[2,128]{1,0:T(2,128)} %bitcast.3, ...), custom_call_target="tpu_custom_call" | custom-call | tf_op jit(solution)/shard_map/pallas_call | solution.py:332
  119.6 0.0 copy-start
  119.6 1.7 %copy.17 = bf16[128,1024]{1,0:T(8,128)(2,1)} copy(bf16[128,1024]{1,0:T(8,128)(2,1)} %get-tuple-element.16) | data formatting | bytes 524288
  121.4 0.0 copy-start.1
  121.4 1.7 %copy.18 = bf16[128,1024]{1,0:T(8,128)(2,1)} copy(bf16[128,1024]{1,0:T(8,128)(2,1)} %get-tuple-element.17) | data formatting | bytes 524288
  123.0 0.0 copy-done.1
  123.1 0.6 copy.19
  123.6 0.0 copy-done
  123.6 0.9 copy.20
Async XLA Ops:
  119.6 4.0 %copy-start = (f32[1,256,768]{2,1,0:T(8,128)S(1)}, f32[1,256,768]{2,1,0:T(8,128)}, u32[]{:S(2)}) copy-start(f32[1,256,768]{2,1,0:T(8,128)} %get-tuple-element.19) | copy-start | bytes 2359300
  121.4 1.7 %copy-start.1 = (f32[2,128]{1,0:T(2,128)S(1)}, f32[2,128]{1,0:T(2,128)}, u32[]{:S(2)}) copy-start(f32[2,128]{1,0:T(2,128)} %get-tuple-element.10) | copy-start | bytes 3076

commit v3 on v2

--- a/solution.py
+++ b/solution.py
@@ -110,17 +110,19 @@
         def _():
             wcopy(m, s, 1, z + 1 + s, z + 1).wait_recv()
 
-    def dsend(finish=False):
-        for s in reversed(range(n - 1)):
-            @pl.when(z + 1 + s <= n - 1)
-            def _():
-                copy = wcopy(2, s, 0, z, z + 1 + s)
-                copy.wait_send() if finish else copy.start()
-
-            @pl.when(z - 1 - s >= 0)
-            def _():
-                copy = wcopy(2, s, 1, z, z - 1 - s)
-                copy.wait_send() if finish else copy.start()
+    at_end = (z == 0) | (z == n - 1)
+    between = (z > 0) & (z < n - 1)
+
+    def dsend(s, where, finish=False):
+        @pl.when(where & (z + 1 + s <= n - 1))
+        def _():
+            copy = wcopy(2, s, 0, z, z + 1 + s)
+            copy.wait_send() if finish else copy.start()
+
+        @pl.when(where & (z - 1 - s >= 0))
+        def _():
+            copy = wcopy(2, s, 1, z, z - 1 - s)
+            copy.wait_send() if finish else copy.start()
 
     for copy in local:
         copy.wait()
@@ -156,8 +158,7 @@
             wrecv(m, s)
             if s + 1 < n - 1:
                 wsend(m, s + 1)
-        if s == max(n - 3, 0):
-            dsend()
+        dsend(s, at_end)
     peers(lambda o, to: acopy(0, o, to).wait_recv())
     peers(lambda o, to: acopy(1, o, to).wait_recv())
 
@@ -171,6 +172,12 @@
         hid[:, c] = (activated * pre_up).astype(BF)
         act[:, c] = activated
         fac[:, c] = pre_up * squashed * (1.0 + pre_gate * (1.0 - squashed))
+
+    for s in range(n - 1):
+        for m in (0, 1):
+            wsend(m, s, finish=True)
+    for s in range(n - 1):
+        dsend(s, between)
 
     def ocopy(j, o, to):
         return pltpu.make_async_remote_copy(
@@ -290,10 +297,9 @@
         total = mm(both, b_cot[j].reshape(slots, depth), 1, 0)
         ft_ref[:, c] = (fg_ref[:, c].astype(F32) + total).astype(BF)
 
-    dsend(finish=True)
-    for s in range(n - 1):
-        for m in (0, 1):
-            wsend(m, s, finish=True)
+    for s in range(n - 1):
+        dsend(s, at_end, finish=True)
+        dsend(s, between, finish=True)
 
         @pl.when(z < n - 1 - s)
         def _():

time: 125 us -> 123 us (0.984)
  the two profiles are of different devices: /device:TPU:0 before, /device:TPU:15 now
where the time goes in v3:
time: 123 us
  Pallas kernels  117 us (95%)
  local copies, waits for them, and re-layouts  4.86 us (4%)
    pallas_call x1, Pallas kernels, per_device(): pl.pallas_call(functools.partial(layer_kernel, n, owners, cap, 1.0 / math...  117 us
    unnamed x8, local copies, waits for them, and re-layouts  4.86 us

profile of v3, /device:TPU:15, one launch (start us, length us, event | category | flops | bytes accessed | tf_op | source)
XLA Modules:
  0.0 123.0 jit_solution(5468882935085577539)
XLA Ops:
  0.6 117.4 %shard_map.120 = (bf16[128,1024]{1,0:T(8,128)(2,1)}, bf16[128,1024]{1,0:T(8,128)(2,1)}, f32[2,128]{1,0:T(2,128)}, f32[1,256,768]{2,1,0:T(8,128)}) custom-call(bf16[128,1024]{1,0:T(8,128)(2,1)} %x_ref.1, bf16[128,1024]{1,0:T(8,128)(2,1)} %so_ref.1, bf16[128,1024]{1,0:T(8,128)(2,1)} %fg_ref.1, bf16[128,1024]{1,0:T(8,128)(2,1)} %sg_ref.1, s32[2,128]{1,0:T(2,128)} %bitcast.3, ...), custom_call_target="tpu_custom_call" | custom-call | tf_op jit(solution)/shard_map/pallas_call | solution.py:338
  118.1 0.0 copy-start
  118.1 1.7 %copy.17 = bf16[128,1024]{1,0:T(8,128)(2,1)} copy(bf16[128,1024]{1,0:T(8,128)(2,1)} %get-tuple-element.16) | data formatting | bytes 524288
  119.8 0.0 copy-start.1
  119.8 1.7 %copy.18 = bf16[128,1024]{1,0:T(8,128)(2,1)} copy(bf16[128,1024]{1,0:T(8,128)(2,1)} %get-tuple-element.17) | data formatting | bytes 524288
  121.5 0.0 copy-done.1
  121.5 0.6 copy.19
  122.1 0.0 copy-done
  122.1 0.9 copy.20
Async XLA Ops:
  118.1 4.0 %copy-start = (f32[1,256,768]{2,1,0:T(8,128)S(1)}, f32[1,256,768]{2,1,0:T(8,128)}, u32[]{:S(2)}) copy-start(f32[1,256,768]{2,1,0:T(8,128)} %get-tuple-element.19) | copy-start | bytes 2359300
  119.8 1.7 %copy-start.1 = (f32[2,128]{1,0:T(2,128)S(1)}, f32[2,128]{1,0:T(2,128)}, u32[]{:S(2)}) copy-start(f32[2,128]{1,0:T(2,128)} %get-tuple-element.10) | copy-start | bytes 3076
